TPU v7x, 32 devices: a whole 2x2x4 slice. The times are simulated.
32 devices in a mesh: replica: 8 (over y, x, core), shard: 4 (over z).
Axes of the slice: x: 2, y: 2, z: 4, core: 2. Of those that a mesh axis runs over, the one named last changes fastest.
Arguments:
- grads: bfloat16 [8, 4, 256, 8192], P('replica', 'shard'), may hold values from -1.25 to 1.25
- master: float32 [256, 8192], P('shard'), may hold values from -0.003 to 0.003
- moment_one: float32 [256, 8192], P('shard'), may hold values from -0.75 to 0.75
- moment_two: float32 [256, 8192], P('shard'), may hold values from 0.005 to 0.2
Outputs:
- master_out: float32 [256, 8192], P('shard')
- moment_one_out: float32 [256, 8192], P('shard')
- moment_two_out: float32 [256, 8192], P('shard')
- weights: bfloat16 [256, 8192], replicated
All inputs are finite; a program needn't handle non-finite values.
Results may differ from a plain program's by a relative error of at most 0.012.
Values may be sent and summed in bfloat16 or wider, within the bound.
A program may use at most 64 MiB of HBM per device.

v0:
```python
import jax
import jax.numpy as jnp
from jax import lax
from jax.sharding import PartitionSpec as P

STEP = 20


def adam_update(total, master, moment_one, moment_two):
    first = 0.9 * moment_one + 0.1 * total
    second = 0.95 * moment_two + 0.05 * total * total
    first_hat = first / (1.0 - 0.9**STEP)
    second_hat = second / (1.0 - 0.95**STEP)
    updated = master - 0.0003 * (first_hat / (jnp.sqrt(second_hat) + 1e-08) + 0.1 * master)
    return (updated, first, second)


def local(grads, master, moment_one, moment_two):
    local_grad = grads[0, 0]
    group_sum = lax.psum_scatter(
        local_grad.astype(jnp.float32).astype(jnp.bfloat16),
        "shard",
        scatter_dimension=0,
        tiled=True,
    ).astype(jnp.float32)
    total = lax.psum(group_sum, "replica")
    updated, first, second = adam_update(total, master, moment_one, moment_two)
    weights = lax.all_gather(updated.astype(jnp.bfloat16), "shard", axis=0, tiled=True)
    return (updated, first, second, weights)


def solution(mesh):
    placed = (
        P("replica", "shard", None, None),
        P("shard", None),
        P("shard", None),
        P("shard", None),
    )
    return jax.shard_map(
        local,
        mesh=mesh,
        in_specs=placed,
        out_specs=(P("shard", None), P("shard", None), P("shard", None), P()),
        check_vma=False,
    )
```

profile of v0, /device:TPU:1, one launch (start us, length us, event | category | flops | bytes accessed | tf_op | source)
XLA Modules:
  0.0 245.7 jit_solution(1162827787167919785)
XLA Ops:
  7.2 0.0 reduce-scatter.2.cloned.1.call-start
  7.2 0.7 reduce-scatter.2.cloned.1.call-update
  7.9 0.0 all-gather.2.cloned.1.call-start
  7.9 81.2 %reduce-scatter.2.cloned.1.call-done = bf16[64,8192]{1,0:T(8,128)(2,1)} async-done(((bf16[256,8192]{1,0:T(8,128)(2,1)}), bf16[64,8192]{1,0:T(8,128)(2,1)}) %reduce-scatter.2.cloned.1.call-update) | async-done | bytes 1048592 | tf_op jit(solution)/shard_map/reduce_scatter | solution.py:20
  89.2 55.7 %all-reduce.1 = f32[64,8192]{1,0:T(8,128)S(1)} all-reduce(bf16[64,8192]{1,0:T(8,128)(2,1)} %reduce-scatter.2.cloned.1.call-done), channel_id=1, replica_groups=mesh['replica'=8,'shard'=4] {'replica'}, use_global_device_ids=true, to_apply=%region_1.0 | all-reduce | flops 524288 | bytes 3145728 | tf_op jit(solution)/shard_map/psum | solution.py:26
  144.9 6.9 %fusion.1 = (bf16[64,8192]{1,0:T(8,128)(2,1)}, f32[64,8192]{1,0:T(8,128)}, f32[64,8192]{1,0:T(8,128)}, f32[64,8192]{1,0:T(8,128)}) fusion(f32[64,8192]{1,0:T(8,128)} %param.5, f32[64,8192]{1,0:T(8,128)S(1)} %all-reduce.1, f32[64,8192]{1,0:T(8,128)} %param.6, f32[64,8192]{1,0:T(8,128)} %param.7), kind=kLoop, calls=%fused_computation.4 | loop fusion | flops 8388608 | bytes 15728640 | tf_op jit(solution)/shard_map/convert_element_type | solution.py:28
  151.9 0.0 all-gather.2.cloned.1.call-update
  151.9 82.4 %all-gather.2.cloned.1.call-done = bf16[256,8192]{1,0:T(8,128)(2,1)} async-done(((bf16[64,8192]{1,0:T(8,128)(2,1)}), bf16[256,8192]{1,0:T(8,128)(2,1)}) %all-gather.2.cloned.1.call-update) | async-done | bytes 4194320 | tf_op jit(solution)/shard_map/all_gather | solution.py:28
  234.2 4.6 %copy.11 = bf16[256,8192]{1,0:T(8,128)(2,1)} copy(bf16[256,8192]{1,0:T(8,128)(2,1)} %all-gather.2.cloned.1.call-done) | data formatting | bytes 8388608
Async XLA Ops:
  7.2 82.0 %reduce-scatter.2.cloned.1.call-start = ((), (), s32[]{:S(2)}) async-start(), calls=%async_computation.1 | async-start | bytes 5242880 | tf_op jit(solution)/shard_map/reduce_scatter | solution.py:20
  7.9 226.3 %all-gather.2.cloned.1.call-start = ((), (), s32[]{:S(2)}) async-start(), calls=%async_computation.2 | async-start | bytes 5242880 | tf_op jit(solution)/shard_map/all_gather | solution.py:28
Sparse Core Ops, SparseCore 0:
  10.3 78.8 reduce-scatter.1
  152.0 82.1 all-gather.1
where the time goes:
time: 247 us; the launch traced here: 246 us
  waiting for transfers between devices  164 us (66%)
  blocking collectives  55.7 us (23%)
  between operations  14 us (6%)
  other arithmetic  6.94 us (3%)
  local copies, waits for them, and re-layouts  4.64 us (2%)
    all_gather x1, waiting for transfers between devices, local(): lax.all_gather(updated.astype(jnp.bfloat16), 'shard', axis=0, tiled=True)  82.4 us
    reduce_scatter x1, waiting for transfers between devices, local(): lax.psum_scatter(local_grad.astype(jnp.float32).astype(jnp.bfloat16), 'sh...  81.2 us
    psum x1, blocking collectives, local(): total = lax.psum(group_sum, 'replica')  55.7 us
    convert_element_type x1, other arithmetic, local(): updated.astype(jnp.bfloat16)  6.94 us
  transfers between devices with their start and end apart: 2, of which 2 were waited for; matrix products, arithmetic and copies ran while one was open for 0% of the time, Pallas kernels for 0%

commit v1 on v0

v1 whole, which is shorter than its diff:
```python
import functools

import jax
import jax.numpy as jnp
from jax import lax
from jax.experimental import pallas as pl
from jax.experimental.pallas import tpu as pltpu
from jax.sharding import PartitionSpec as P

STEP = 20
MESH = pl.DeviceIdType.MESH


def adam_update(total, master, moment_one, moment_two):
    first = 0.9 * moment_one + 0.1 * total
    second = 0.95 * moment_two + 0.05 * total * total
    first_hat = first / (1.0 - 0.9**STEP)
    second_hat = second / (1.0 - 0.95**STEP)
    updated = master - 0.0003 * (first_hat / (jnp.sqrt(second_hat) + 1e-08) + 0.1 * master)
    return (updated, first, second)


def aligned(offset, width):
    return pl.ds(pl.multiple_of(offset, width), width)


def over_tiles(rows, columns, body):
    width = min(columns, 1024)
    across = columns // width

    def step(index, carry):
        row = pl.multiple_of(index // across * 16, 16)
        body(pl.ds(row, 16), pl.multiple_of(index % across * width, width), width)
        return carry

    lax.fori_loop(0, rows // 16 * across, step, 0)


def kernel(replicas, shards, grads, master, moment_one, moment_two, total_out, weights_out, *scratch):
    stages = replicas.bit_length() - 2
    own, theirs, from_shard, held, old_master, old_one, old_two = scratch[:7]
    arrived = scratch[7 : 7 + stages]
    summed = scratch[7 + stages : 7 + 2 * stages]
    (
        load_sem, state_sem, store_sem, core_send, core_recv, halve_send, halve_recv, shard_send, shard_recv,
        spread_send, spread_recv, join_send, join_recv, pair_send, pair_recv,
    ) = scratch[7 + 2 * stages :]

    rows = master.shape[0]
    columns = master.shape[1]
    half = columns // 2
    stream = half // 2
    me = lax.axis_index("replica")
    at = lax.axis_index("shard")
    bit = [me // (1 << b) % 2 for b in range(stages + 1)]
    partner = [me + (1 - 2 * bit[b]) * (1 << b) for b in range(stages + 1)]
    forward = list(range(1, stages + 1))
    orders = (forward, forward[::-1])

    def width(stage):
        return stream >> (stage + 1)

    def base(q, stage):
        offset = q * stream
        for u in range(stage + 1):
            offset = offset + bit[orders[q][u]] * width(u)
        return offset

    def remote(src, dst, send_sem, recv_sem, replica, shard):
        copy = pltpu.make_async_remote_copy(
            src_ref=src, dst_ref=dst, send_sem=send_sem, recv_sem=recv_sem,
            device_id=(replica, shard), device_id_type=MESH,
        )
        copy.start()
        return copy

    sent = []
    local = []

    loads = []
    for i in range(shards):
        block = lax.rem(at + 1 + i, shards)
        copy = pltpu.make_async_copy(
            grads.at[0, 0, aligned(block * rows, rows), aligned(bit[0] * half, half)], own.at[i], load_sem.at[i]
        )
        copy.start()
        loads.append(copy)
    states = []
    for s, (source, target) in enumerate(((master, old_master), (moment_one, old_one), (moment_two, old_two))):
        for q in range(2):
            offset = bit[0] * half + base(q, stages - 1)
            copy = pltpu.make_async_copy(
                source.at[:, aligned(offset, width(stages - 1))], target.at[q], state_sem.at[s, q]
            )
            copy.start()
            states.append(copy)

    barrier = pltpu.get_barrier_semaphore()
    for other in partner:
        pl.semaphore_signal(barrier, inc=1, device_id=(other, at), device_id_type=MESH)
    for d in range(1, shards):
        pl.semaphore_signal(barrier, inc=1, device_id=(me, lax.rem(at + d, shards)), device_id_type=MESH)
    pl.semaphore_wait(barrier, len(partner) + shards - 1)

    core = []
    for i in range(shards):
        block = lax.rem(at + 1 + i, shards)
        core.append(
            remote(
                grads.at[0, 0, aligned(block * rows, rows), aligned((1 - bit[0]) * half, half)],
                theirs.at[i], core_send.at[i], core_recv.at[i], partner[0], at,
            )
        )
    sent += core
    halving = {}
    shard_copies = []

    def start_halving(i, stage):
        for q in range(2):
            wide = width(stage)
            b = orders[q][stage]
            if stage == 0:
                source = own.at[i, :, aligned(q * stream + (1 - bit[b]) * wide, wide)]
            else:
                source = summed[stage - 1].at[i, q, :, aligned((1 - bit[b]) * wide, wide)]
            halving[i, stage, q] = remote(
                source, arrived[stage].at[i, q], halve_send.at[i, stage, q], halve_recv.at[i, stage, q], partner[b], at
            )
            sent.append(halving[i, stage, q])

    def phase(i, step):
        if step == 0:
            loads[i].wait()
            core[i].wait_recv()

            def add(r, c, wide):
                mine = own[i, r, pl.ds(c, wide)].astype(jnp.float32)
                own[i, r, pl.ds(c, wide)] = (mine + theirs[i, r, pl.ds(c, wide)].astype(jnp.float32)).astype(jnp.bfloat16)

            over_tiles(rows, half, add)
            start_halving(i, 0)
            return
        stage = step - 1
        for q in range(2):
            halving[i, stage, q].wait_recv()
            kept = bit[orders[q][stage]] * width(stage)

            def add(r, c, wide):
                if stage == 0:
                    mine = own[i, r, pl.ds(pl.multiple_of(q * stream + kept + c, wide), wide)]
                else:
                    mine = summed[stage - 1][i, q, r, pl.ds(pl.multiple_of(kept + c, wide), wide)]
                other = arrived[stage][i, q, r, pl.ds(c, wide)]
                summed[stage][i, q, r, pl.ds(c, wide)] = (
                    mine.astype(jnp.float32) + other.astype(jnp.float32)
                ).astype(jnp.bfloat16)

            over_tiles(rows, width(stage), add)
        if step < stages:
            start_halving(i, step)
        elif i < shards - 1:
            copy = remote(
                summed[stages - 1].at[i], from_shard.at[i], shard_send.at[i], shard_recv.at[i],
                me, lax.rem(at + 1 + i, shards),
            )
            shard_copies.append(copy)
            sent.append(copy)

    for tick in range(shards + stages):
        for step in range(stages + 1):
            if 0 <= tick - step < shards:
                phase(tick - step, step)

    for copy in states:
        copy.wait()
    for copy in shard_copies:
        copy.wait_recv()
    piece = width(stages - 1)
    for q in range(2):
        offset = base(q, stages - 1)

        def update(r, c, wide):
            total = summed[stages - 1][shards - 1, q, r, pl.ds(c, wide)].astype(jnp.float32)
            for i in range(shards - 1):
                total = total + from_shard[i, q, r, pl.ds(c, wide)].astype(jnp.float32)
            rounded = total.astype(jnp.bfloat16)
            where = pl.ds(pl.multiple_of(offset + c, wide), wide)
            held[1, r, where] = rounded
            updated, _, _ = adam_update(
                rounded.astype(jnp.float32), old_master[q, r, pl.ds(c, wide)],
                old_one[q, r, pl.ds(c, wide)], old_two[q, r, pl.ds(c, wide)],
            )
            held[0, r, where] = updated.astype(jnp.bfloat16)

        over_tiles(rows, piece, update)

    spread = {}
    for d in range(1, shards):
        for q in range(2):
            where = aligned(base(q, stages - 1), piece)
            spread[d, q] = remote(
                held.at[0, :, where], held.at[1 + d, :, where], spread_send.at[d - 1, q], spread_recv.at[d - 1, q],
                me, lax.rem(at + d, shards),
            )
            sent.append(spread[d, q])
    joining = {}
    pairs = []

    def join(j, stage):
        for q in range(2):
            where = aligned(base(q, stage), width(stage))
            joining[j, stage, q] = remote(
                held.at[j, :, where], held.at[j, :, where], join_send.at[j, stage, q], join_recv.at[j, stage, q],
                partner[orders[q][stage]], at,
            )
            sent.append(joining[j, stage, q])

    def gather(j, step):
        if step == 0:
            if j > 1:
                for q in range(2):
                    spread[j - 1, q].wait_recv()
        else:
            for q in range(2):
                joining[j, stages - step, q].wait_recv()
        if step < stages:
            join(j, stages - 1 - step)
            return
        if j == 1:
            target = total_out.at[:, aligned(bit[0] * half, half)]
        else:
            block = at if j == 0 else lax.rem(at + shards - (j - 1), shards)
            target = weights_out.at[aligned(block * rows, rows), aligned(bit[0] * half, half)]
        pair = remote(held.at[j], target, pair_send.at[j], pair_recv.at[j], partner[0], at)
        pairs.append(pair)
        sent.append(pair)
        copy = pltpu.make_async_copy(held.at[j], target, store_sem.at[j])
        copy.start()
        local.append(copy)

    for tick in range(shards + 1 + stages):
        for step in range(stages + 1):
            if 0 <= tick - step < shards + 1:
                gather(tick - step, step)

    for copy in pairs:
        copy.wait_recv()
    for copy in local:
        copy.wait()
    for copy in sent:
        copy.wait_send()


def local(replicas, shards, grads, master, moment_one, moment_two):
    rows, columns = master.shape
    half = columns // 2
    stages = replicas.bit_length() - 2
    piece = half // 2 >> stages
    halves = [(shards, 2, rows, half // 2 >> (t + 1)) for t in range(stages)]
    sem = pltpu.SemaphoreType.DMA
    total, weights = pl.pallas_call(
        functools.partial(kernel, replicas, shards),
        out_shape=(
            jax.ShapeDtypeStruct((rows, columns), jnp.bfloat16),
            jax.ShapeDtypeStruct((rows * shards, columns), jnp.bfloat16),
        ),
        in_specs=[pl.BlockSpec(memory_space=pl.ANY)] * 4,
        out_specs=[pl.BlockSpec(memory_space=pl.ANY)] * 2,
        scratch_shapes=[
            pltpu.VMEM((shards, rows, half), jnp.bfloat16),
            pltpu.VMEM((shards, rows, half), jnp.bfloat16),
            pltpu.VMEM((shards - 1, 2, rows, piece), jnp.bfloat16),
            pltpu.VMEM((shards + 1, rows, half), jnp.bfloat16),
            *[pltpu.VMEM((2, rows, piece), jnp.float32)] * 3,
            *[pltpu.VMEM(shape, jnp.bfloat16) for shape in halves * 2],
            sem((shards,)),
            sem((3, 2)),
            sem((shards + 1,)),
            *[sem((shards,))] * 2,
            *[sem((shards, stages, 2))] * 2,
            *[sem((shards - 1,))] * 2,
            *[sem((shards - 1, 2))] * 2,
            *[sem((shards + 1, stages, 2))] * 2,
            *[sem((shards + 1,))] * 2,
        ],
        compiler_params=pltpu.CompilerParams(
            collective_id=0, has_side_effects=True, vmem_limit_bytes=24 * 1024 * 1024
        ),
        name="reduce_update_gather",
    )(grads, master, moment_one, moment_two)
    updated, first, second = adam_update(total.astype(jnp.float32), master, moment_one, moment_two)
    return (updated, first, second, weights)


def solution(mesh):
    placed = (
        P("replica", "shard", None, None),
        P("shard", None),
        P("shard", None),
        P("shard", None),
    )
    return jax.shard_map(
        functools.partial(local, mesh.shape["replica"], mesh.shape["shard"]),
        mesh=mesh,
        in_specs=placed,
        out_specs=(P("shard", None), P("shard", None), P("shard", None), P()),
        check_vma=False,
    )
```

time: 247 us -> 71.6 us (0.29)
  waiting for transfers between devices: 164 us -> 0 us
  Pallas kernels: 0 us -> 57.7 us
  blocking collectives: 55.7 us -> 0 us
  between operations: 14 us -> 0.68 us
  local copies, waits for them, and re-layouts: 4.64 us -> 8.98 us
  other arithmetic: 6.94 us -> 3.77 us
    all_gather x1 -> x0, waiting for transfers between devices: 82.4 us -> none  [local(): lax.all_gather(updated.astype(jnp.bfloat16), 'shard', axis=0, tiled=True)]
    reduce_scatter x1 -> x0, waiting for transfers between devices: 81.2 us -> none  [local(): lax.psum_scatter(local_grad.astype(jnp.float32).astype(jnp.bfloat16), 'sh...]
    pallas_call x0 -> x1, Pallas kernels: none -> 57.7 us  [local(): pl.pallas_call(functools.partial(kernel, replicas, shards), out_shape=(ja...]
    psum x1 -> x0, blocking collectives: 55.7 us -> none  [local(): total = lax.psum(group_sum, 'replica')]
    convert_element_type x1 -> x0, other arithmetic: 6.94 us -> none  [local(): updated.astype(jnp.bfloat16)]
    unnamed x1 -> x15, local copies, waits for them, and re-layouts: 4.64 us -> 8.98 us
    sub x0 -> x1, other arithmetic: none -> 3.77 us  [adam_update(): master - 0.0003 * (first_hat / (jnp.sqrt(second_hat) + 1e-08) + 0.1 * mas...]
  transfers between devices with their start and end apart: 2 -> 0, of which waited for: 2 -> 0; matrix products, arithmetic and copies ran while one was open for 0% -> 0% of each run, Pallas kernels for 0% -> 0%
where the time goes in v1:
time: 71.6 us; the launch traced here: 71.1 us
  Pallas kernels  57.7 us (81%)
  local copies, waits for them, and re-layouts  8.98 us (13%)
  other arithmetic  3.77 us (5%)
    pallas_call x1, Pallas kernels, local(): pl.pallas_call(functools.partial(kernel, replicas, shards), out_shape=(ja...  57.7 us
    unnamed x15, local copies, waits for them, and re-layouts  8.98 us
    sub x1, other arithmetic, adam_update(): master - 0.0003 * (first_hat / (jnp.sqrt(second_hat) + 1e-08) + 0.1 * mas...  3.77 us

profile of v1, /device:TPU:1, one launch (start us, length us, event | category | flops | bytes accessed | tf_op | source)
XLA Modules:
  0.0 71.1 jit_solution(12138186585384441985)
XLA Ops:
  0.6 0.0 copy-start
  0.6 1.6 %copy-done = f32[64,8192]{1,0:T(8,128)S(1)} copy-done((f32[64,8192]{1,0:T(8,128)S(1)}, f32[64,8192]{1,0:T(8,128)}, u32[]{:S(2)}) %copy-start) | copy-done | bytes 2097176
  2.2 0.0 copy-start.2
  2.2 1.6 %copy-done.2 = f32[64,8192]{1,0:T(8,128)S(1)} copy-done((f32[64,8192]{1,0:T(8,128)S(1)}, f32[64,8192]{1,0:T(8,128)}, u32[]{:S(2)}) %copy-start.2) | copy-done | bytes 2097176
  3.8 0.0 copy-start.4
  3.8 1.6 %copy-done.4 = f32[64,8192]{1,0:T(8,128)S(1)} copy-done((f32[64,8192]{1,0:T(8,128)S(1)}, f32[64,8192]{1,0:T(8,128)}, u32[]{:S(2)}) %copy-start.4) | copy-done | bytes 2097176
  5.4 0.0 copy-start.6
  5.4 2.2 %copy-done.6 = bf16[1,1,256,8192]{3,2,1,0:T(8,128)(2,1)S(1)} copy-done((bf16[1,1,256,8192]{3,2,1,0:T(8,128)(2,1)S(1)}, bf16[1,1,256,8192]{3,2,1,0:T(8,128)(2,1)}, u32[]{:S(2)}) %copy-start.6) | copy-done | bytes 4194328
  7.6 0.0 copy-start.1
  7.6 0.0 copy-start.3
  7.6 0.0 copy-start.5
  7.6 57.7 %reduce_update_gather.1 = (bf16[64,8192]{1,0:T(8,128)(2,1)S(1)}, bf16[256,8192]{1,0:T(8,128)(2,1)S(1)}) custom-call(bf16[1,1,256,8192]{3,2,1,0:T(8,128)(2,1)S(1)} %copy-done.6, f32[64,8192]{1,0:T(8,128)S(1)} %copy-done, f32[64,8192]{1,0:T(8,128)S(1)} %copy-done.2, f32[64,8192]{1,0:T(8,128)S(1)} %copy-done.4), custom_call_target="tpu_custom_call" | custom-call | tf_op jit(solution)/shard_map/reduce_update_gather/pallas_call | solution.py:261
  65.3 0.0 copy-done.1
  65.3 0.0 copy-done.3
  65.3 0.0 copy-done.5
  65.3 3.8 %multiply_subtract_fusion = (f32[64,8192]{1,0:T(8,128)}, f32[64,8192]{1,0:T(8,128)}, f32[64,8192]{1,0:T(8,128)}) fusion(f32[64,8192]{1,0:T(8,128)S(1)} %copy-done.1, bf16[64,8192]{1,0:T(8,128)(2,1)S(1)} %get-tuple-element.6, f32[64,8192]{1,0:T(8,128)S(1)} %copy-done.3, f32[64,8192]{1,0:T(8,128)S(1)} %copy-done.5), kind=kLoop, calls=%fused_computation.4 | loop fusion | flops 8388608 | bytes 13631488 | tf_op jit(solution)/shard_map/sub | solution.py:19
  69.1 2.0 %copy.9 = bf16[256,8192]{1,0:T(8,128)(2,1)} copy(bf16[256,8192]{1,0:T(8,128)(2,1)S(1)} %get-tuple-element.18) | data formatting | bytes 8388608
Async XLA Ops:
  0.6 1.6 %copy-start = (f32[64,8192]{1,0:T(8,128)S(1)}, f32[64,8192]{1,0:T(8,128)}, u32[]{:S(2)}) copy-start(f32[64,8192]{1,0:T(8,128)} %master.1) | copy-start | bytes 6291460
  2.2 1.6 %copy-start.2 = (f32[64,8192]{1,0:T(8,128)S(1)}, f32[64,8192]{1,0:T(8,128)}, u32[]{:S(2)}) copy-start(f32[64,8192]{1,0:T(8,128)} %moment_one.1) | copy-start | bytes 6291460
  3.8 1.6 %copy-start.4 = (f32[64,8192]{1,0:T(8,128)S(1)}, f32[64,8192]{1,0:T(8,128)}, u32[]{:S(2)}) copy-start(f32[64,8192]{1,0:T(8,128)} %moment_two.1) | copy-start | bytes 6291460
  5.4 2.2 %copy-start.6 = (bf16[1,1,256,8192]{3,2,1,0:T(8,128)(2,1)S(1)}, bf16[1,1,256,8192]{3,2,1,0:T(8,128)(2,1)}, u32[]{:S(2)}) copy-start(bf16[1,1,256,8192]{3,2,1,0:T(8,128)(2,1)} %grads.1) | copy-start | bytes 12582916
  7.6 57.7 %copy-start.1 = (f32[64,8192]{1,0:T(8,128)S(1)}, f32[64,8192]{1,0:T(8,128)}, u32[]{:S(2)}) copy-start(f32[64,8192]{1,0:T(8,128)} %master.1) | copy-start | bytes 6291460
  7.6 57.7 %copy-start.3 = (f32[64,8192]{1,0:T(8,128)S(1)}, f32[64,8192]{1,0:T(8,128)}, u32[]{:S(2)}) copy-start(f32[64,8192]{1,0:T(8,128)} %moment_one.1) | copy-start | bytes 6291460
  7.6 57.7 %copy-start.5 = (f32[64,8192]{1,0:T(8,128)S(1)}, f32[64,8192]{1,0:T(8,128)}, u32[]{:S(2)}) copy-start(f32[64,8192]{1,0:T(8,128)} %moment_two.1) | copy-start | bytes 6291460

commit v2 on v1

v2 whole, which is shorter than its diff:
```python
import functools

import jax
import jax.numpy as jnp
from jax import lax
from jax.experimental import pallas as pl
from jax.experimental.pallas import tpu as pltpu
from jax.sharding import PartitionSpec as P

STEP = 20
MESH = pl.DeviceIdType.MESH


def adam_update(total, master, moment_one, moment_two):
    first = 0.9 * moment_one + 0.1 * total
    second = 0.95 * moment_two + 0.05 * total * total
    first_hat = first / (1.0 - 0.9**STEP)
    second_hat = second / (1.0 - 0.95**STEP)
    updated = master - 0.0003 * (first_hat / (jnp.sqrt(second_hat) + 1e-08) + 0.1 * master)
    return (updated, first, second)


def aligned(offset, width):
    return pl.ds(pl.multiple_of(offset, width), width)


def over_tiles(rows, columns, body, widest=2048):
    width = min(columns, widest)
    across = columns // width

    def step(index, carry):
        row = pl.multiple_of(index // across * 16, 16)
        body(pl.ds(row, 16), pl.multiple_of(index % across * width, width), width)
        return carry

    lax.fori_loop(0, rows // 16 * across, step, 0)


def kernel(
    replicas, shards, grads, master, moment_one, moment_two,
    master_out, one_out, two_out, weights_out, *scratch,
):
    stages = replicas.bit_length() - 2
    (
        own, theirs, from_shard, held, total_pair, own_weights, row_weights, all_master, all_one, all_two,
    ) = scratch[:10]
    arrived = scratch[10 : 10 + stages]
    summed = scratch[10 + stages : 10 + 2 * stages]
    (
        load_sem, state_sem, store_sem, out_sem, core_send, core_recv, halve_send, halve_recv, shard_send, shard_recv,
        spread_send, spread_recv, join_send, join_recv, pair_send, pair_recv,
    ) = scratch[10 + 2 * stages :]

    rows = master.shape[0]
    columns = master.shape[1]
    half = columns // 2
    stream = half // 2
    me = lax.axis_index("replica")
    at = lax.axis_index("shard")
    bit = [me // (1 << b) % 2 for b in range(stages + 1)]
    partner = [me + (1 - 2 * bit[b]) * (1 << b) for b in range(stages + 1)]
    forward = list(range(1, stages + 1))
    orders = (forward, forward[::-1])

    def width(stage):
        return stream >> (stage + 1)

    def base(q, stage):
        offset = q * stream
        for u in range(stage + 1):
            offset = offset + bit[orders[q][u]] * width(u)
        return offset

    def remote(src, dst, send_sem, recv_sem, replica, shard):
        copy = pltpu.make_async_remote_copy(
            src_ref=src, dst_ref=dst, send_sem=send_sem, recv_sem=recv_sem,
            device_id=(replica, shard), device_id_type=MESH,
        )
        copy.start()
        return copy

    sent = []
    local = []

    loads = []
    for i in range(shards):
        block = lax.rem(at + 1 + i, shards)
        copy = pltpu.make_async_copy(
            grads.at[0, 0, aligned(block * rows, rows), aligned(bit[0] * half, half)], own.at[i], load_sem.at[i]
        )
        copy.start()
        loads.append(copy)
    barrier = pltpu.get_barrier_semaphore()
    for other in partner:
        pl.semaphore_signal(barrier, inc=1, device_id=(other, at), device_id_type=MESH)
    for d in range(1, shards):
        pl.semaphore_signal(barrier, inc=1, device_id=(me, lax.rem(at + d, shards)), device_id_type=MESH)
    pl.semaphore_wait(barrier, len(partner) + shards - 1)

    core = []

    def start_core(i):
        block = lax.rem(at + 1 + i, shards)
        core.append(
            remote(
                grads.at[0, 0, aligned(block * rows, rows), aligned((1 - bit[0]) * half, half)],
                theirs.at[i], core_send.at[i], core_recv.at[i], partner[0], at,
            )
        )
        sent.append(core[i])

    for i in range(2):
        start_core(i)
    states = []
    for s, (source, target) in enumerate(((master, all_master), (moment_one, all_one), (moment_two, all_two))):
        copy = pltpu.make_async_copy(source, target, state_sem.at[s])
        copy.start()
        states.append(copy)
    halving = {}
    shard_copies = []

    def start_halving(i, stage, q):
        wide = width(stage)
        b = orders[q][stage]
        if stage == 0:
            source = own.at[i, :, aligned(q * stream + (1 - bit[b]) * wide, wide)]
        else:
            source = summed[stage - 1].at[i, q, :, aligned((1 - bit[b]) * wide, wide)]
        halving[i, stage, q] = remote(
            source, arrived[stage].at[i, q], halve_send.at[i, stage, q], halve_recv.at[i, stage, q], partner[b], at
        )
        sent.append(halving[i, stage, q])

    def phase(i, step):
        if step == 0:
            loads[i].wait()
            core[i].wait_recv()
            if i + 2 < shards:
                start_core(i + 2)
            for q in range(2):

                def add(r, c, wide):
                    where = pl.ds(pl.multiple_of(q * stream + c, wide), wide)
                    own[i, r, where] = own[i, r, where] + theirs[i, r, where]

                over_tiles(rows, stream, add)
                start_halving(i, 0, q)
            return
        stage = step - 1
        for q in range(2):
            halving[i, stage, q].wait_recv()
            kept = bit[orders[q][stage]] * width(stage)

            def add(r, c, wide):
                if stage == 0:
                    mine = own[i, r, pl.ds(pl.multiple_of(q * stream + kept + c, wide), wide)]
                else:
                    mine = summed[stage - 1][i, q, r, pl.ds(pl.multiple_of(kept + c, wide), wide)]
                summed[stage][i, q, r, pl.ds(c, wide)] = mine + arrived[stage][i, q, r, pl.ds(c, wide)]

            over_tiles(rows, width(stage), add)
            if step < stages:
                start_halving(i, step, q)
        if step == stages and i < shards - 1:
            copy = remote(
                summed[stages - 1].at[i], from_shard.at[i], shard_send.at[i], shard_recv.at[i],
                me, lax.rem(at + 1 + i, shards),
            )
            shard_copies.append(copy)
            sent.append(copy)

    for tick in range(shards + stages):
        for step in range(stages + 1):
            if 0 <= tick - step < shards:
                phase(tick - step, step)

    for copy in states:
        copy.wait()
    for copy in shard_copies:
        copy.wait_recv()
    piece = width(stages - 1)
    for q in range(2):
        offset = base(q, stages - 1)

        def finish(r, c, wide):
            total = summed[stages - 1][shards - 1, q, r, pl.ds(c, wide)].astype(jnp.float32)
            for i in range(shards - 1):
                total = total + from_shard[i, q, r, pl.ds(c, wide)].astype(jnp.float32)
            rounded = total.astype(jnp.bfloat16)
            held[0, r, pl.ds(pl.multiple_of(offset + c, wide), wide)] = rounded
            where = pl.ds(pl.multiple_of(bit[0] * half + offset + c, wide), wide)
            updated, _, _ = adam_update(
                rounded.astype(jnp.float32), all_master[r, where], all_one[r, where], all_two[r, where]
            )
            own_weights[q, r, pl.ds(c, wide)] = updated.astype(jnp.bfloat16)

        over_tiles(rows, piece, finish, 512)

    spread = {}
    for d in range(1, shards):
        for q in range(2):
            spread[d, q] = remote(
                own_weights.at[q], held.at[d, :, aligned(base(q, stages - 1), piece)],
                spread_send.at[d - 1, q], spread_recv.at[d - 1, q], me, lax.rem(at + d, shards),
            )
            sent.append(spread[d, q])
    joining = {}
    pairs = []
    todo = []

    def join(j, stage, q):
        where = aligned(base(q, stage), width(stage))
        joining[j, stage, q] = remote(
            held.at[j, :, where], held.at[j, :, where], join_send.at[j, stage, q], join_recv.at[j, stage, q],
            partner[orders[q][stage]], at,
        )
        sent.append(joining[j, stage, q])

    def update_rows(side, group):
        start = (bit[0] if side == 0 else 1 - bit[0]) * half
        if side == 1 and group == 0:
            pairs[0].wait_recv()

        def update(r, c, wide):
            r = pl.ds(group * 16, 16)
            total = held[0, r, pl.ds(c, wide)] if side == 0 else total_pair[r, pl.ds(c, wide)]
            where = pl.ds(pl.multiple_of(start + c, wide), wide)
            updated, first, second = adam_update(
                total.astype(jnp.float32), all_master[r, where], all_one[r, where], all_two[r, where]
            )
            all_master[r, where] = updated
            all_one[r, where] = first
            all_two[r, where] = second
            row_weights[r, where] = updated.astype(jnp.bfloat16)

        over_tiles(16, half, update, 512)
        if group == rows // 16 - 1:
            where = aligned(start, half)
            targets = (
                (all_master, master_out.at[:, where]),
                (all_one, one_out.at[:, where]),
                (all_two, two_out.at[:, where]),
                (row_weights, weights_out.at[aligned(at * rows, rows), where]),
            )
            for s, (source, target) in enumerate(targets):
                copy = pltpu.make_async_copy(source.at[:, where], target, out_sem.at[side, s])
                copy.start()
                local.append(copy)

    def gather(j, step):
        for q in range(2):
            if step > 0:
                joining[j, stages - step, q].wait_recv()
            elif j > 0:
                spread[j, q].wait_recv()
            if step < stages:
                join(j, stages - 1 - step, q)
        if step < stages:
            return
        if j == 0:
            pair = remote(held.at[0], total_pair, pair_send.at[0], pair_recv.at[0], partner[0], at)
            todo.extend((side, group) for side in range(2) for group in range(rows // 16))
        else:
            block = lax.rem(at + shards - j, shards)
            target = weights_out.at[aligned(block * rows, rows), aligned(bit[0] * half, half)]
            pair = remote(held.at[j], target, pair_send.at[j], pair_recv.at[j], partner[0], at)
            copy = pltpu.make_async_copy(held.at[j], target, store_sem.at[j - 1])
            copy.start()
            local.append(copy)
        pairs.append(pair)
        sent.append(pair)

    for tick in range(shards + stages):
        for step in range(stages + 1):
            if 0 <= tick - step < shards:
                gather(tick - step, step)
                if todo:
                    update_rows(*todo.pop(0))
    while todo:
        update_rows(*todo.pop(0))

    for copy in pairs[1:]:
        copy.wait_recv()
    for copy in local:
        copy.wait()
    for copy in sent:
        copy.wait_send()


def write_out(*refs):
    count = len(refs) // 2
    copies = [pltpu.make_async_copy(refs[k], refs[count + k], refs[-1].at[k]) for k in range(count)]
    for copy in copies:
        copy.start()
    for copy in copies:
        copy.wait()


def local(replicas, shards, grads, master, moment_one, moment_two):
    rows, columns = master.shape
    half = columns // 2
    stages = replicas.bit_length() - 2
    piece = half // 2 >> stages
    halves = [(shards, 2, rows, half // 2 >> (t + 1)) for t in range(stages)]
    sem = pltpu.SemaphoreType.DMA
    hbm = pl.BlockSpec(memory_space=pltpu.HBM)
    outs = tuple(
        jax.ShapeDtypeStruct(shape, dtype)
        for shape, dtype in [((rows, columns), jnp.float32)] * 3 + [((rows * shards, columns), jnp.bfloat16)]
    )
    results = pl.pallas_call(
        functools.partial(kernel, replicas, shards),
        out_shape=outs,
        in_specs=[hbm] * 4,
        out_specs=[pl.BlockSpec(memory_space=pl.ANY)] * 4,
        scratch_shapes=[
            pltpu.VMEM((shards, rows, half), jnp.bfloat16),
            pltpu.VMEM((shards, rows, half), jnp.bfloat16),
            pltpu.VMEM((shards - 1, 2, rows, piece), jnp.bfloat16),
            pltpu.VMEM((shards, rows, half), jnp.bfloat16),
            pltpu.VMEM((rows, half), jnp.bfloat16),
            pltpu.VMEM((2, rows, piece), jnp.bfloat16),
            pltpu.VMEM((rows, columns), jnp.bfloat16),
            *[pltpu.VMEM((rows, columns), jnp.float32)] * 3,
            *[pltpu.VMEM(shape, jnp.bfloat16) for shape in halves * 2],
            sem((shards,)),
            sem((3,)),
            sem((shards - 1,)),
            sem((2, 4)),
            *[sem((shards,))] * 2,
            *[sem((shards, stages, 2))] * 2,
            *[sem((shards - 1,))] * 2,
            *[sem((shards - 1, 2))] * 2,
            *[sem((shards, stages, 2))] * 2,
            *[sem((shards,))] * 2,
        ],
        compiler_params=pltpu.CompilerParams(
            collective_id=0, has_side_effects=True, vmem_limit_bytes=28 * 1024 * 1024
        ),
        name="reduce_update_gather",
    )(*(pltpu.with_memory_space_constraint(x, pltpu.HBM) for x in (grads, master, moment_one, moment_two)))
    return pl.pallas_call(
        write_out,
        out_shape=outs,
        in_specs=[pl.BlockSpec(memory_space=pl.ANY)] * 4,
        out_specs=[hbm] * 4,
        scratch_shapes=[sem((4,))],
        name="write_out",
    )(*results)


def solution(mesh):
    placed = (
        P("replica", "shard", None, None),
        P("shard", None),
        P("shard", None),
        P("shard", None),
    )
    return jax.shard_map(
        functools.partial(local, mesh.shape["replica"], mesh.shape["shard"]),
        mesh=mesh,
        in_specs=placed,
        out_specs=(P("shard", None), P("shard", None), P("shard", None), P()),
        check_vma=False,
    )
```

time: 71.6 us -> 383 us (5.35)
  Pallas kernels: 57.7 us -> 376 us
    pallas_call x1 -> x2, Pallas kernels: 57.7 us -> 376 us  [the longest x1 319 us: local(): pl.pallas_call(write_out, out_shape=outs, in_specs=[pl.BlockSpec(memory_s...]
    unnamed x15 -> x8, local copies, waits for them, and re-layouts: 8.98 us -> 5.94 us
where the time goes in v2:
time: 383 us
  Pallas kernels  376 us (98%)
  local copies, waits for them, and re-layouts  5.94 us (2%)
    pallas_call x1, Pallas kernels, local(): pl.pallas_call(write_out, out_shape=outs, in_specs=[pl.BlockSpec(memory_s...  319 us
    pallas_call x1, Pallas kernels, local(): pl.pallas_call(functools.partial(kernel, replicas, shards), out_shape=out...  57.2 us

profile of v2, /device:TPU:1, one launch (start us, length us, event | category | flops | bytes accessed | tf_op | source)
XLA Modules:
  0.0 382.6 jit_solution(13808378155254526138)
XLA Ops:
  0.6 57.2 %reduce_update_gather.1 = (f32[64,8192]{1,0:T(8,128)S(1)}, f32[64,8192]{1,0:T(8,128)S(1)}, f32[64,8192]{1,0:T(8,128)S(1)}, bf16[256,8192]{1,0:T(8,128)(2,1)S(1)}) custom-call(bf16[1,1,256,8192]{3,2,1,0:T(8,128)(2,1)} %grads.1, f32[64,8192]{1,0:T(8,128)} %master.1, f32[64,8192]{1,0:T(8,128)} %moment_one.1, f32[64,8192]{1,0:T(8,128)} %moment_two.1), custom_call_target="tpu_custom_call" | custom-call | tf_op jit(solution)/shard_map/reduce_update_gather/pallas_call | solution.py:311
  57.9 0.0 copy-start
  57.9 1.9 copy-done
  59.8 0.0 copy-start.1
  59.8 1.3 copy-done.1
  61.1 0.0 copy-start.2
  61.1 1.3 copy-done.2
  62.5 0.0 copy-start.3
  62.5 1.3 copy-done.3
  63.8 318.8 %write_out.1 = (f32[64,8192]{1,0:T(8,128)}, f32[64,8192]{1,0:T(8,128)}, f32[64,8192]{1,0:T(8,128)}, bf16[256,8192]{1,0:T(8,128)(2,1)}) custom-call(f32[64,8192]{1,0:T(8,128)} %copy-done.1, f32[64,8192]{1,0:T(8,128)} %copy-done.2, f32[64,8192]{1,0:T(8,128)} %copy-done.3, bf16[256,8192]{1,0:T(8,128)(2,1)} %copy-done), custom_call_target="tpu_custom_call" | custom-call | tf_op jit(solution)/shard_map/write_out/pallas_call | solution.py:342
Async XLA Ops:
  57.9 1.9 copy-start
  59.8 1.3 copy-start.1
  61.1 1.3 copy-start.2
  62.5 1.3 copy-start.3

commit v3 on v2

--- a/solution.py
+++ b/solution.py
@@ -174,36 +174,9 @@
             if 0 <= tick - step < shards:
                 phase(tick - step, step)
 
-    for copy in states:
-        copy.wait()
     for copy in shard_copies:
         copy.wait_recv()
     piece = width(stages - 1)
-    for q in range(2):
-        offset = base(q, stages - 1)
-
-        def finish(r, c, wide):
-            total = summed[stages - 1][shards - 1, q, r, pl.ds(c, wide)].astype(jnp.float32)
-            for i in range(shards - 1):
-                total = total + from_shard[i, q, r, pl.ds(c, wide)].astype(jnp.float32)
-            rounded = total.astype(jnp.bfloat16)
-            held[0, r, pl.ds(pl.multiple_of(offset + c, wide), wide)] = rounded
-            where = pl.ds(pl.multiple_of(bit[0] * half + offset + c, wide), wide)
-            updated, _, _ = adam_update(
-                rounded.astype(jnp.float32), all_master[r, where], all_one[r, where], all_two[r, where]
-            )
-            own_weights[q, r, pl.ds(c, wide)] = updated.astype(jnp.bfloat16)
-
-        over_tiles(rows, piece, finish, 512)
-
-    spread = {}
-    for d in range(1, shards):
-        for q in range(2):
-            spread[d, q] = remote(
-                own_weights.at[q], held.at[d, :, aligned(base(q, stages - 1), piece)],
-                spread_send.at[d - 1, q], spread_recv.at[d - 1, q], me, lax.rem(at + d, shards),
-            )
-            sent.append(spread[d, q])
     joining = {}
     pairs = []
     todo = []
@@ -215,6 +188,41 @@
             partner[orders[q][stage]], at,
         )
         sent.append(joining[j, stage, q])
+
+    for q in range(2):
+        offset = base(q, stages - 1)
+
+        def finish(r, c, wide):
+            total = summed[stages - 1][shards - 1, q, r, pl.ds(c, wide)].astype(jnp.float32)
+            for i in range(shards - 1):
+                total = total + from_shard[i, q, r, pl.ds(c, wide)].astype(jnp.float32)
+            held[0, r, pl.ds(pl.multiple_of(offset + c, wide), wide)] = total.astype(jnp.bfloat16)
+
+        over_tiles(rows, piece, finish, 512)
+        join(0, stages - 1, q)
+
+    for copy in states:
+        copy.wait()
+    for q in range(2):
+        offset = base(q, stages - 1)
+
+        def own_update(r, c, wide):
+            total = held[0, r, pl.ds(pl.multiple_of(offset + c, wide), wide)].astype(jnp.float32)
+            where = pl.ds(pl.multiple_of(bit[0] * half + offset + c, wide), wide)
+            updated, _, _ = adam_update(total, all_master[r, where], all_one[r, where], all_two[r, where])
+            own_weights[q, r, pl.ds(c, wide)] = updated.astype(jnp.bfloat16)
+
+        over_tiles(rows, piece, own_update, 512)
+
+    spread = {}
+
+    def start_spread(d):
+        for q in range(2):
+            spread[d, q] = remote(
+                own_weights.at[q], held.at[d, :, aligned(base(q, stages - 1), piece)],
+                spread_send.at[d - 1, q], spread_recv.at[d - 1, q], me, lax.rem(at + d, shards),
+            )
+            sent.append(spread[d, q])
 
     def update_rows(side, group):
         start = (bit[0] if side == 0 else 1 - bit[0]) * half
@@ -253,7 +261,7 @@
                 joining[j, stages - step, q].wait_recv()
             elif j > 0:
                 spread[j, q].wait_recv()
-            if step < stages:
+            if step < stages and (j, step) != (0, 0):
                 join(j, stages - 1 - step, q)
         if step < stages:
             return
@@ -271,11 +279,13 @@
         sent.append(pair)
 
     for tick in range(shards + stages):
-        for step in range(stages + 1):
-            if 0 <= tick - step < shards:
-                gather(tick - step, step)
-                if todo:
-                    update_rows(*todo.pop(0))
+        steps = [step for step in reversed(range(stages + 1)) if 0 <= tick - step < shards]
+        for place, step in enumerate(steps):
+            gather(tick - step, step)
+            if place == 0 and tick + 1 < shards:
+                start_spread(tick + 1)
+            if todo:
+                update_rows(*todo.pop(0))
     while todo:
         update_rows(*todo.pop(0))
 
@@ -342,9 +352,10 @@
     return pl.pallas_call(
         write_out,
         out_shape=outs,
-        in_specs=[pl.BlockSpec(memory_space=pl.ANY)] * 4,
+        in_specs=[pl.BlockSpec(memory_space=pltpu.VMEM)] * 4,
         out_specs=[hbm] * 4,
         scratch_shapes=[sem((4,))],
+        compiler_params=pltpu.CompilerParams(vmem_limit_bytes=16 * 1024 * 1024),
         name="write_out",
     )(*results)
 

time: 383 us -> 65.1 us (0.17)
  Pallas kernels: 376 us -> 64.3 us
  local copies, waits for them, and re-layouts: 5.94 us -> 0 us
    pallas_call x1, Pallas kernels: 319 us -> 4.06 us  [local(): pl.pallas_call(write_out, out_shape=outs, in_specs=[pl.BlockSpec(memory_s...]
    unnamed x8 -> x0, local copies, waits for them, and re-layouts: 5.94 us -> none
where the time goes in v3:
time: 65.1 us; the launch traced here: 65 us
  Pallas kernels  64.3 us (99%)
    pallas_call x1, Pallas kernels, local(): pl.pallas_call(functools.partial(kernel, replicas, shards), out_shape=out...  60.3 us
    pallas_call x1, Pallas kernels, local(): pl.pallas_call(write_out, out_shape=outs, in_specs=[pl.BlockSpec(memory_s...  4.06 us

profile of v3, /device:TPU:1, one launch (start us, length us, event | category | flops | bytes accessed | tf_op | source)
XLA Modules:
  0.0 65.0 jit_solution(1016189224132264482)
XLA Ops:
  0.6 60.3 %reduce_update_gather.1 = (f32[64,8192]{1,0:T(8,128)S(1)}, f32[64,8192]{1,0:T(8,128)S(1)}, f32[64,8192]{1,0:T(8,128)S(1)}, bf16[256,8192]{1,0:T(8,128)(2,1)S(1)}) custom-call(bf16[1,1,256,8192]{3,2,1,0:T(8,128)(2,1)} %grads.1, f32[64,8192]{1,0:T(8,128)} %master.1, f32[64,8192]{1,0:T(8,128)} %moment_one.1, f32[64,8192]{1,0:T(8,128)} %moment_two.1), custom_call_target="tpu_custom_call" | custom-call | tf_op jit(solution)/shard_map/reduce_update_gather/pallas_call | solution.py:321
  60.9 4.1 %write_out.1 = (f32[64,8192]{1,0:T(8,128)}, f32[64,8192]{1,0:T(8,128)}, f32[64,8192]{1,0:T(8,128)}, bf16[256,8192]{1,0:T(8,128)(2,1)}) custom-call(f32[64,8192]{1,0:T(8,128)S(1)} %get-tuple-element.8.refs_0_, f32[64,8192]{1,0:T(8,128)S(1)} %get-tuple-element.9.refs_1_, f32[64,8192]{1,0:T(8,128)S(1)} %get-tuple-element.10.refs_2_, ...), custom_call_target="tpu_custom_call" | custom-call | tf_op jit(solution)/shard_map/write_out/pallas_call | solution.py:352

commit v4 on v2

v4 whole, which is shorter than its diff:
```python
import functools

import jax
import jax.numpy as jnp
from jax import lax
from jax.experimental import pallas as pl
from jax.experimental.pallas import tpu as pltpu
from jax.sharding import PartitionSpec as P

STEP = 20
MESH = pl.DeviceIdType.MESH


def adam_update(total, master, moment_one, moment_two):
    first = 0.9 * moment_one + 0.1 * total
    second = 0.95 * moment_two + 0.05 * total * total
    first_hat = first / (1.0 - 0.9**STEP)
    second_hat = second / (1.0 - 0.95**STEP)
    updated = master - 0.0003 * (first_hat / (jnp.sqrt(second_hat) + 1e-08) + 0.1 * master)
    return (updated, first, second)


def aligned(offset, width):
    return pl.ds(pl.multiple_of(offset, width), width)


def over_tiles(rows, columns, body, widest=2048):
    width = min(columns, widest)
    across = columns // width

    def step(index, carry):
        body(pl.multiple_of(index // across * 16, 16), pl.multiple_of(index % across * width, width), width)
        return carry

    lax.fori_loop(0, rows // 16 * across, step, 0)


def kernel(
    replicas, shards, parts, grads, master, moment_one, moment_two,
    master_out, one_out, two_out, weights_out, *scratch,
):
    stages = replicas.bit_length() - 2
    (
        own, theirs, from_shard, held, total_pair, own_weights, row_weights, all_master, all_one, all_two,
    ) = scratch[:10]
    arrived = scratch[10 : 10 + stages]
    summed = scratch[10 + stages : 10 + 2 * stages]
    (
        load_sem, state_sem, store_sem, out_sem, core_send, core_recv, halve_send, halve_recv, shard_send, shard_recv,
        spread_send, spread_recv, join_send, join_recv, pair_send, pair_recv,
    ) = scratch[10 + 2 * stages :]

    rows = master.shape[0] // parts
    columns = master.shape[1]
    half = columns // 2
    stream = half // 2
    chunks = parts * shards
    me = lax.axis_index("replica")
    at = lax.axis_index("shard")
    bit = [me // (1 << b) % 2 for b in range(stages + 1)]
    partner = [me + (1 - 2 * bit[b]) * (1 << b) for b in range(stages + 1)]
    forward = list(range(1, stages + 1))
    orders = (forward, forward[::-1])

    def width(stage):
        return stream >> (stage + 1)

    def base(q, stage):
        offset = q * stream
        for u in range(stage + 1):
            offset = offset + bit[orders[q][u]] * width(u)
        return offset

    def remote(src, dst, send_sem, recv_sem, replica, shard):
        copy = pltpu.make_async_remote_copy(
            src_ref=src, dst_ref=dst, send_sem=send_sem, recv_sem=recv_sem,
            device_id=(replica, shard), device_id_type=MESH,
        )
        copy.start()
        return copy

    def tile(row, offset=0):
        return pl.ds(pl.multiple_of(row + offset, 16), 16)

    def span(offset, column, wide):
        return pl.ds(pl.multiple_of(offset + column, wide), wide)

    sent = []
    local = []

    def chunk_rows(part, shard):
        return aligned((shard * parts + part) * rows, rows)

    def reduced_rows(n):
        return chunk_rows(n // shards, lax.rem(at + 1 + n % shards, shards))

    loads = []
    for n in range(chunks):
        copy = pltpu.make_async_copy(
            grads.at[0, 0, reduced_rows(n), aligned(bit[0] * half, half)], own.at[n], load_sem.at[n]
        )
        copy.start()
        loads.append(copy)

    barrier = pltpu.get_barrier_semaphore()
    for other in partner:
        pl.semaphore_signal(barrier, inc=1, device_id=(other, at), device_id_type=MESH)
    for d in range(1, shards):
        pl.semaphore_signal(barrier, inc=1, device_id=(me, lax.rem(at + d, shards)), device_id_type=MESH)
    pl.semaphore_wait(barrier, len(partner) + shards - 1)

    core = []

    def start_core(n):
        core.append(
            remote(
                grads.at[0, 0, reduced_rows(n), aligned((1 - bit[0]) * half, half)],
                theirs.at[n], core_send.at[n], core_recv.at[n], partner[0], at,
            )
        )
        sent.append(core[n])

    for n in range(2):
        start_core(n)
    states = []
    for s, (source, target) in enumerate(((master, all_master), (moment_one, all_one), (moment_two, all_two))):
        copy = pltpu.make_async_copy(source, target, state_sem.at[s])
        copy.start()
        states.append(copy)
    halving = {}
    shard_copies = {part: [] for part in range(parts)}

    def start_halving(n, stage, q):
        wide = width(stage)
        b = orders[q][stage]
        if stage == 0:
            source = own.at[n, :, aligned(q * stream + (1 - bit[b]) * wide, wide)]
        else:
            source = summed[stage - 1].at[n, q, :, aligned((1 - bit[b]) * wide, wide)]
        halving[n, stage, q] = remote(
            source, arrived[stage].at[n, q], halve_send.at[n, stage, q], halve_recv.at[n, stage, q], partner[b], at
        )
        sent.append(halving[n, stage, q])

    def reduce(n, step):
        if step == 0:
            loads[n].wait()
            core[n].wait_recv()
            if n + 2 < chunks:
                start_core(n + 2)
            for q in range(2):

                def add(r, c, wide):
                    where = span(q * stream, c, wide)
                    own[n, tile(r), where] = own[n, tile(r), where] + theirs[n, tile(r), where]

                over_tiles(rows, stream, add)
                start_halving(n, 0, q)
            return
        stage = step - 1
        for q in range(2):
            halving[n, stage, q].wait_recv()
            kept = bit[orders[q][stage]] * width(stage)

            def add(r, c, wide):
                if stage == 0:
                    mine = own[n, tile(r), span(q * stream + kept, c, wide)]
                else:
                    mine = summed[stage - 1][n, q, tile(r), span(kept, c, wide)]
                summed[stage][n, q, tile(r), pl.ds(c, wide)] = mine + arrived[stage][n, q, tile(r), pl.ds(c, wide)]

            over_tiles(rows, width(stage), add)
            if step < stages:
                start_halving(n, step, q)
        part, i = divmod(n, shards)
        if step == stages and i < shards - 1:
            copy = remote(
                summed[stages - 1].at[n], from_shard.at[part, i], shard_send.at[part, i], shard_recv.at[part, i],
                me, lax.rem(at + 1 + i, shards),
            )
            shard_copies[part].append(copy)
            sent.append(copy)

    piece = width(stages - 1)
    joining = {}
    spread = {}
    pairs = {}
    todo = []

    def join(m, stage, q):
        where = aligned(base(q, stage), width(stage))
        joining[m, stage, q] = remote(
            held.at[m, :, where], held.at[m, :, where], join_send.at[m, stage, q], join_recv.at[m, stage, q],
            partner[orders[q][stage]], at,
        )
        sent.append(joining[m, stage, q])

    def own_piece(part):
        for copy in shard_copies[part]:
            copy.wait_recv()
        m = part * shards
        for q in range(2):
            offset = base(q, stages - 1)

            def finish(r, c, wide):
                total = summed[stages - 1][m + shards - 1, q, tile(r), pl.ds(c, wide)].astype(jnp.float32)
                for i in range(shards - 1):
                    total = total + from_shard[part, i, q, tile(r), pl.ds(c, wide)].astype(jnp.float32)
                held[m, tile(r), span(offset, c, wide)] = total.astype(jnp.bfloat16)

            over_tiles(rows, piece, finish, 512)
            join(m, stages - 1, q)
        if part == 0:
            for copy in states:
                copy.wait()
        for q in range(2):
            offset = base(q, stages - 1)

            def own_update(r, c, wide):
                total = held[m, tile(r), span(offset, c, wide)].astype(jnp.float32)
                row = tile(r, part * rows)
                where = span(bit[0] * half + offset, c, wide)
                updated, _, _ = adam_update(total, all_master[row, where], all_one[row, where], all_two[row, where])
                own_weights[part, q, tile(r), pl.ds(c, wide)] = updated.astype(jnp.bfloat16)

            over_tiles(rows, piece, own_update, 512)
        for d in range(1, shards):
            for q in range(2):
                spread[part, d, q] = remote(
                    own_weights.at[part, q], held.at[m + d, :, aligned(base(q, stages - 1), piece)],
                    spread_send.at[part, d - 1, q], spread_recv.at[part, d - 1, q], me, lax.rem(at + d, shards),
                )
                sent.append(spread[part, d, q])

    def update_rows(part, side, group):
        start = (bit[0] if side == 0 else 1 - bit[0]) * half
        m = part * shards
        if side == 1 and group == 0:
            pairs[m].wait_recv()

        def update(r, c, wide):
            r = pl.ds(group * 16, 16)
            total = held[m, r, pl.ds(c, wide)] if side == 0 else total_pair[part, r, pl.ds(c, wide)]
            row = pl.ds(part * rows + group * 16, 16)
            where = span(start, c, wide)
            updated, first, second = adam_update(
                total.astype(jnp.float32), all_master[row, where], all_one[row, where], all_two[row, where]
            )
            all_master[row, where] = updated
            all_one[row, where] = first
            all_two[row, where] = second
            row_weights[row, where] = updated.astype(jnp.bfloat16)

        over_tiles(16, half, update, 512)
        if group == rows // 16 - 1:
            block = pl.ds(part * rows, rows)
            where = aligned(start, half)
            targets = (
                (all_master, master_out.at[block, where]),
                (all_one, one_out.at[block, where]),
                (all_two, two_out.at[block, where]),
                (row_weights, weights_out.at[chunk_rows(part, at), where]),
            )
            for s, (source, target) in enumerate(targets):
                copy = pltpu.make_async_copy(source.at[block, where], target, out_sem.at[part, side, s])
                copy.start()
                local.append(copy)

    def gather(m, step):
        part, j = divmod(m, shards)
        for q in range(2):
            if step > 0:
                joining[m, stages - step, q].wait_recv()
            elif j > 0:
                spread[part, j, q].wait_recv()
            if step < stages and (j, step) != (0, 0):
                join(m, stages - 1 - step, q)
        if step < stages:
            return
        if j == 0:
            target = total_pair.at[part]
            todo.extend((part, side, group) for side in range(2) for group in range(rows // 16))
        else:
            target = weights_out.at[
                chunk_rows(part, lax.rem(at + shards - j, shards)), aligned(bit[0] * half, half)
            ]
            copy = pltpu.make_async_copy(held.at[m], target, store_sem.at[m])
            copy.start()
            local.append(copy)
        pairs[m] = remote(held.at[m], target, pair_send.at[m], pair_recv.at[m], partner[0], at)
        sent.append(pairs[m])

    ahead = 2

    def gather_tick(tick):
        for step in reversed(range(stages + 1)):
            if 0 <= tick - step * ahead < chunks:
                gather(tick - step * ahead, step)
                if todo:
                    update_rows(*todo.pop(0))

    ready = 0
    gathered = 0
    for tick in range(chunks + stages):
        for step in range(stages + 1):
            if 0 <= tick - step < chunks:
                reduce(tick - step, step)
        if tick == (ready + 1) * shards - 1 + stages:
            own_piece(ready)
            ready += 1
        if gathered < ready * shards:
            gather_tick(gathered)
            gathered += 1
    while gathered < chunks + stages * ahead:
        gather_tick(gathered)
        gathered += 1
    while todo:
        update_rows(*todo.pop(0))

    for m, pair in pairs.items():
        if m % shards:
            pair.wait_recv()
    for copy in local:
        copy.wait()
    for copy in sent:
        copy.wait_send()


def write_out(*refs):
    count = len(refs) // 2
    copies = [pltpu.make_async_copy(refs[k], refs[count + k], refs[-1].at[k]) for k in range(count)]
    for copy in copies:
        copy.start()
    for copy in copies:
        copy.wait()


def local(replicas, shards, grads, master, moment_one, moment_two):
    rows, columns = master.shape
    half = columns // 2
    stages = replicas.bit_length() - 2
    piece = half // 2 >> stages
    parts = 2 if rows % 32 == 0 else 1
    chunks = parts * shards
    part = rows // parts
    halves = [(chunks, 2, part, half // 2 >> (t + 1)) for t in range(stages)]
    sem = pltpu.SemaphoreType.DMA
    hbm = pl.BlockSpec(memory_space=pltpu.HBM)
    outs = tuple(
        jax.ShapeDtypeStruct(shape, dtype)
        for shape, dtype in [((rows, columns), jnp.float32)] * 3 + [((rows * shards, columns), jnp.bfloat16)]
    )
    results = pl.pallas_call(
        functools.partial(kernel, replicas, shards, parts),
        out_shape=outs,
        in_specs=[hbm] * 4,
        out_specs=[pl.BlockSpec(memory_space=pl.ANY)] * 4,
        scratch_shapes=[
            pltpu.VMEM((chunks, part, half), jnp.bfloat16),
            pltpu.VMEM((chunks, part, half), jnp.bfloat16),
            pltpu.VMEM((parts, shards - 1, 2, part, piece), jnp.bfloat16),
            pltpu.VMEM((chunks, part, half), jnp.bfloat16),
            pltpu.VMEM((parts, part, half), jnp.bfloat16),
            pltpu.VMEM((parts, 2, part, piece), jnp.bfloat16),
            pltpu.VMEM((rows, columns), jnp.bfloat16),
            *[pltpu.VMEM((rows, columns), jnp.float32)] * 3,
            *[pltpu.VMEM(shape, jnp.bfloat16) for shape in halves * 2],
            sem((chunks,)),
            sem((3,)),
            sem((chunks,)),
            sem((parts, 2, 4)),
            *[sem((chunks,))] * 2,
            *[sem((chunks, stages, 2))] * 2,
            *[sem((parts, shards - 1))] * 2,
            *[sem((parts, shards - 1, 2))] * 2,
            *[sem((chunks, stages, 2))] * 2,
            *[sem((chunks,))] * 2,
        ],
        compiler_params=pltpu.CompilerParams(
            collective_id=0, has_side_effects=True, vmem_limit_bytes=28 * 1024 * 1024
        ),
        name="reduce_update_gather",
    )(*(pltpu.with_memory_space_constraint(x, pltpu.HBM) for x in (grads, master, moment_one, moment_two)))
    return pl.pallas_call(
        write_out,
        out_shape=outs,
        in_specs=[pl.BlockSpec(memory_space=pltpu.VMEM)] * 4,
        out_specs=[hbm] * 4,
        scratch_shapes=[sem((4,))],
        compiler_params=pltpu.CompilerParams(vmem_limit_bytes=16 * 1024 * 1024),
        name="write_out",
    )(*results)


def solution(mesh):
    placed = (
        P("replica", "shard", None, None),
        P("shard", None),
        P("shard", None),
        P("shard", None),
    )
    return jax.shard_map(
        functools.partial(local, mesh.shape["replica"], mesh.shape["shard"]),
        mesh=mesh,
        in_specs=placed,
        out_specs=(P("shard", None), P("shard", None), P("shard", None), P()),
        check_vma=False,
    )
```

time: 383 us -> 59.7 us (0.16)
  Pallas kernels: 376 us -> 58.9 us
  local copies, waits for them, and re-layouts: 5.94 us -> 0 us
    pallas_call x1, Pallas kernels: 319 us -> 4.06 us  [local(): pl.pallas_call(write_out, out_shape=outs, in_specs=[pl.BlockSpec(memory_s...]
    unnamed x8 -> x0, local copies, waits for them, and re-layouts: 5.94 us -> none
where the time goes in v4:
time: 59.7 us; the launch traced here: 59.6 us
  Pallas kernels  58.9 us (99%)
  between operations  0.64 us (1%)
    pallas_call x1, Pallas kernels, local(): pl.pallas_call(functools.partial(kernel, replicas, shards, parts), out_sh...  54.9 us
    pallas_call x1, Pallas kernels, local(): pl.pallas_call(write_out, out_shape=outs, in_specs=[pl.BlockSpec(memory_s...  4.06 us

profile of v4, /device:TPU:1, one launch (start us, length us, event | category | flops | bytes accessed | tf_op | source)
XLA Modules:
  0.0 59.6 jit_solution(4775017550416975997)
XLA Ops:
  0.6 54.9 %reduce_update_gather.1 = (f32[64,8192]{1,0:T(8,128)S(1)}, f32[64,8192]{1,0:T(8,128)S(1)}, f32[64,8192]{1,0:T(8,128)S(1)}, bf16[256,8192]{1,0:T(8,128)(2,1)S(1)}) custom-call(bf16[1,1,256,8192]{3,2,1,0:T(8,128)(2,1)} %grads.1, f32[64,8192]{1,0:T(8,128)} %master.1, f32[64,8192]{1,0:T(8,128)} %moment_one.1, f32[64,8192]{1,0:T(8,128)} %moment_two.1), custom_call_target="tpu_custom_call" | custom-call | tf_op jit(solution)/shard_map/reduce_update_gather/pallas_call | solution.py:353
  55.5 4.1 %write_out.1 = (f32[64,8192]{1,0:T(8,128)}, f32[64,8192]{1,0:T(8,128)}, f32[64,8192]{1,0:T(8,128)}, bf16[256,8192]{1,0:T(8,128)(2,1)}) custom-call(f32[64,8192]{1,0:T(8,128)S(1)} %get-tuple-element.8.refs_0_, f32[64,8192]{1,0:T(8,128)S(1)} %get-tuple-element.9.refs_1_, f32[64,8192]{1,0:T(8,128)S(1)} %get-tuple-element.10.refs_2_, ...), custom_call_target="tpu_custom_call" | custom-call | tf_op jit(solution)/shard_map/write_out/pallas_call | solution.py:384

commit v5 on v4

--- a/solution.py
+++ b/solution.py
@@ -33,6 +33,93 @@
         return carry
 
     lax.fori_loop(0, rows // 16 * across, step, 0)
+
+
+CORE_AHEAD = 2
+
+
+def plan(shards, stages, parts, groups, kib, hop=1.5, rate=100.0, issue=0.1):
+    chunks = parts * shards
+    now, free, arrives = 2.0, {}, {}
+    left = [shards] * parts
+
+    def send(key, link, amount, speed):
+        nonlocal now
+        now += issue
+        free[link] = max(now, free.get(link, 0.0)) + amount * 1.024 / speed
+        arrives[key] = free[link] + hop
+
+    def core(n):
+        if n < chunks:
+            send(("core", n), "core", kib, 6 * rate)
+
+    def needs(kind, n, step):
+        if kind == "reduce":
+            return [("core", n)] if step == 0 else [("halve", n, step - 1, q) for q in range(2)]
+        if kind == "own":
+            return [("shard", n, i) for i in range(shards - 1)]
+        if kind == "gather":
+            return [("spread", n)] if step == 0 else [("join", n, step - 1, q) for q in range(2)]
+        return [("pair", n * shards)] if step else []
+
+    def take(kind, n, step):
+        nonlocal now
+        if kind == "reduce":
+            if step == 0:
+                core(n + CORE_AHEAD)
+            for q in range(2):
+                now += 0.4 / parts / 2**step
+                if step < stages:
+                    send(("halve", n, step, q), (q + step) % stages, kib / 2 ** (step + 1), rate)
+            if step < stages:
+                return [("reduce", n, step + 1)]
+            part, i = divmod(n, shards)
+            left[part] -= 1
+            if i < shards - 1:
+                send(("shard", part, i), "shard", min(i + 1, shards - 1 - i) * kib / 2**stages, rate)
+            return [] if left[part] else [("own", part, 0)]
+        if kind == "own":
+            for q in range(2):
+                now += 0.2 / parts
+                send(("join", n * shards, 0, q), (q + stages - 1) % stages, kib / 2**stages, rate)
+            now += 0.8 / parts
+            for d in range(1, shards):
+                send(("spread", n * shards + d), "shard", min(d, shards - d) * kib / 2**stages, rate)
+            return [("gather", n * shards, 1)] + [("gather", n * shards + d, 0) for d in range(1, shards)]
+        if kind == "gather":
+            if step < stages:
+                for q in range(2):
+                    send(("join", n, step, q), (q + stages - 1 - step) % stages, kib / 2 ** (stages - step), rate)
+                return [("gather", n, step + 1)]
+            send(("pair", n), "core", kib, 6 * rate)
+            if n % shards:
+                return []
+            return [("update", n // shards, side, group) for side in range(2) for group in range(groups)]
+        now += 0.5
+        return []
+
+    for n in range(CORE_AHEAD):
+        core(n)
+    ready = [("reduce", n, 0) for n in range(chunks)]
+    order = []
+    while ready:
+        best = None
+        for op in ready:
+            waits = needs(*op[:3])
+            if any(key not in arrives for key in waits):
+                continue
+            start = max([now] + [arrives[key] for key in waits])
+            if op[0] == "update":
+                place = (start + 0.5, 2, op[1:])
+            else:
+                place = (start, 1 if op[0] == "gather" else 0, (op[1], -op[2]))
+            if best is None or place < best[0]:
+                best = (place, start, op)
+        now = best[1]
+        ready.remove(best[2])
+        order.append(best[2])
+        ready += take(*best[2][:3])
+    return order
 
 
 def kernel(
@@ -109,18 +196,16 @@
         pl.semaphore_signal(barrier, inc=1, device_id=(me, lax.rem(at + d, shards)), device_id_type=MESH)
     pl.semaphore_wait(barrier, len(partner) + shards - 1)
 
-    core = []
+    core = {}
 
     def start_core(n):
-        core.append(
-            remote(
-                grads.at[0, 0, reduced_rows(n), aligned((1 - bit[0]) * half, half)],
-                theirs.at[n], core_send.at[n], core_recv.at[n], partner[0], at,
-            )
+        core[n] = remote(
+            grads.at[0, 0, reduced_rows(n), aligned((1 - bit[0]) * half, half)],
+            theirs.at[n], core_send.at[n], core_recv.at[n], partner[0], at,
         )
         sent.append(core[n])
 
-    for n in range(2):
+    for n in range(CORE_AHEAD):
         start_core(n)
     states = []
     for s, (source, target) in enumerate(((master, all_master), (moment_one, all_one), (moment_two, all_two))):
@@ -146,8 +231,8 @@
         if step == 0:
             loads[n].wait()
             core[n].wait_recv()
-            if n + 2 < chunks:
-                start_core(n + 2)
+            if n + CORE_AHEAD < chunks:
+                start_core(n + CORE_AHEAD)
             for q in range(2):
 
                 def add(r, c, wide):
@@ -185,7 +270,6 @@
     joining = {}
     spread = {}
     pairs = {}
-    todo = []
 
     def join(m, stage, q):
         where = aligned(base(q, stage), width(stage))
@@ -195,7 +279,7 @@
         )
         sent.append(joining[m, stage, q])
 
-    def own_piece(part):
+    def own_piece(part, step):
         for copy in shard_copies[part]:
             copy.wait_recv()
         m = part * shards
@@ -210,9 +294,8 @@
 
             over_tiles(rows, piece, finish, 512)
             join(m, stages - 1, q)
-        if part == 0:
-            for copy in states:
-                copy.wait()
+        while states:
+            states.pop().wait()
         for q in range(2):
             offset = base(q, stages - 1)
 
@@ -271,15 +354,14 @@
         for q in range(2):
             if step > 0:
                 joining[m, stages - step, q].wait_recv()
-            elif j > 0:
+            else:
                 spread[part, j, q].wait_recv()
-            if step < stages and (j, step) != (0, 0):
+            if step < stages:
                 join(m, stages - 1 - step, q)
         if step < stages:
             return
         if j == 0:
             target = total_pair.at[part]
-            todo.extend((part, side, group) for side in range(2) for group in range(rows // 16))
         else:
             target = weights_out.at[
                 chunk_rows(part, lax.rem(at + shards - j, shards)), aligned(bit[0] * half, half)
@@ -290,32 +372,10 @@
         pairs[m] = remote(held.at[m], target, pair_send.at[m], pair_recv.at[m], partner[0], at)
         sent.append(pairs[m])
 
-    ahead = 2
-
-    def gather_tick(tick):
-        for step in reversed(range(stages + 1)):
-            if 0 <= tick - step * ahead < chunks:
-                gather(tick - step * ahead, step)
-                if todo:
-                    update_rows(*todo.pop(0))
-
-    ready = 0
-    gathered = 0
-    for tick in range(chunks + stages):
-        for step in range(stages + 1):
-            if 0 <= tick - step < chunks:
-                reduce(tick - step, step)
-        if tick == (ready + 1) * shards - 1 + stages:
-            own_piece(ready)
-            ready += 1
-        if gathered < ready * shards:
-            gather_tick(gathered)
-            gathered += 1
-    while gathered < chunks + stages * ahead:
-        gather_tick(gathered)
-        gathered += 1
-    while todo:
-        update_rows(*todo.pop(0))
+    steps = {"reduce": reduce, "own": own_piece, "gather": gather, "update": update_rows}
+    kib = rows * half * 2 // 1024
+    for kind, *which in plan(shards, stages, parts, rows // 16, kib):
+        steps[kind](*which)
 
     for m, pair in pairs.items():
         if m % shards:

time: 59.7 us -> 61.3 us (1.027)
  Pallas kernels: 58.9 us -> 60.2 us
    pallas_call x1, Pallas kernels: 54.9 us -> 56.2 us  [local(): pl.pallas_call(functools.partial(kernel, replicas, shards, parts), out_sh...]
where the time goes in v5:
time: 61.3 us; the launch traced here: 60.9 us
  Pallas kernels  60.2 us (98%)
  between operations  0.64 us (1%)
    pallas_call x1, Pallas kernels, local(): pl.pallas_call(functools.partial(kernel, replicas, shards, parts), out_sh...  56.2 us
    pallas_call x1, Pallas kernels, local(): pl.pallas_call(write_out, out_shape=outs, in_specs=[pl.BlockSpec(memory_s...  4.06 us

profile of v5, /device:TPU:1, one launch (start us, length us, event | category | flops | bytes accessed | tf_op | source)
XLA Modules:
  0.0 60.9 jit_solution(257955177612249343)
XLA Ops:
  0.6 56.2 %reduce_update_gather.1 = (f32[64,8192]{1,0:T(8,128)S(1)}, f32[64,8192]{1,0:T(8,128)S(1)}, f32[64,8192]{1,0:T(8,128)S(1)}, bf16[256,8192]{1,0:T(8,128)(2,1)S(1)}) custom-call(bf16[1,1,256,8192]{3,2,1,0:T(8,128)(2,1)} %grads.1, f32[64,8192]{1,0:T(8,128)} %master.1, f32[64,8192]{1,0:T(8,128)} %moment_one.1, f32[64,8192]{1,0:T(8,128)} %moment_two.1), custom_call_target="tpu_custom_call" | custom-call | tf_op jit(solution)/shard_map/reduce_update_gather/pallas_call | solution.py:413
  56.8 4.1 %write_out.1 = (f32[64,8192]{1,0:T(8,128)}, f32[64,8192]{1,0:T(8,128)}, f32[64,8192]{1,0:T(8,128)}, bf16[256,8192]{1,0:T(8,128)(2,1)}) custom-call(f32[64,8192]{1,0:T(8,128)S(1)} %get-tuple-element.8.refs_0_, f32[64,8192]{1,0:T(8,128)S(1)} %get-tuple-element.9.refs_1_, f32[64,8192]{1,0:T(8,128)S(1)} %get-tuple-element.10.refs_2_, ...), custom_call_target="tpu_custom_call" | custom-call | tf_op jit(solution)/shard_map/write_out/pallas_call | solution.py:444

commit v6 on v4

--- a/solution.py
+++ b/solution.py
@@ -13,10 +13,11 @@
 
 def adam_update(total, master, moment_one, moment_two):
     first = 0.9 * moment_one + 0.1 * total
-    second = 0.95 * moment_two + 0.05 * total * total
-    first_hat = first / (1.0 - 0.9**STEP)
-    second_hat = second / (1.0 - 0.95**STEP)
-    updated = master - 0.0003 * (first_hat / (jnp.sqrt(second_hat) + 1e-08) + 0.1 * master)
+    second = 0.95 * moment_two + 0.05 * (total * total)
+    second_hat = second * (1.0 / (1.0 - 0.95**STEP))
+    root = second_hat * lax.rsqrt(second_hat)
+    step = (0.0003 / (1.0 - 0.9**STEP)) * first / (root + 1e-08)
+    updated = (1.0 - 0.0003 * 0.1) * master - step
     return (updated, first, second)
 
 
@@ -208,7 +209,7 @@
                     total = total + from_shard[part, i, q, tile(r), pl.ds(c, wide)].astype(jnp.float32)
                 held[m, tile(r), span(offset, c, wide)] = total.astype(jnp.bfloat16)
 
-            over_tiles(rows, piece, finish, 512)
+            over_tiles(rows, piece, finish)
             join(m, stages - 1, q)
         if part == 0:
             for copy in states:
@@ -223,7 +224,7 @@
                 updated, _, _ = adam_update(total, all_master[row, where], all_one[row, where], all_two[row, where])
                 own_weights[part, q, tile(r), pl.ds(c, wide)] = updated.astype(jnp.bfloat16)
 
-            over_tiles(rows, piece, own_update, 512)
+            over_tiles(rows, piece, own_update)
         for d in range(1, shards):
             for q in range(2):
                 spread[part, d, q] = remote(
@@ -232,17 +233,18 @@
                 )
                 sent.append(spread[part, d, q])
 
-    def update_rows(part, side, group):
+    def update_rows(part, side, group, place):
         start = (bit[0] if side == 0 else 1 - bit[0]) * half
         m = part * shards
-        if side == 1 and group == 0:
+        if side == 1 and group == 0 and place == 0:
             pairs[m].wait_recv()
 
         def update(r, c, wide):
             r = pl.ds(group * 16, 16)
-            total = held[m, r, pl.ds(c, wide)] if side == 0 else total_pair[part, r, pl.ds(c, wide)]
+            here = span(place * stream, c, wide)
+            total = held[m, r, here] if side == 0 else total_pair[part, r, here]
             row = pl.ds(part * rows + group * 16, 16)
-            where = span(start, c, wide)
+            where = span(start + place * stream, c, wide)
             updated, first, second = adam_update(
                 total.astype(jnp.float32), all_master[row, where], all_one[row, where], all_two[row, where]
             )
@@ -251,8 +253,8 @@
             all_two[row, where] = second
             row_weights[row, where] = updated.astype(jnp.bfloat16)
 
-        over_tiles(16, half, update, 512)
-        if group == rows // 16 - 1:
+        over_tiles(16, stream, update, 1024)
+        if group == rows // 16 - 1 and place == 1:
             block = pl.ds(part * rows, rows)
             where = aligned(start, half)
             targets = (
@@ -279,7 +281,9 @@
             return
         if j == 0:
             target = total_pair.at[part]
-            todo.extend((part, side, group) for side in range(2) for group in range(rows // 16))
+            todo.extend(
+                (part, side, group, place) for side in range(2) for group in range(rows // 16) for place in range(2)
+            )
         else:
             target = weights_out.at[
                 chunk_rows(part, lax.rem(at + shards - j, shards)), aligned(bit[0] * half, half)

time: 59.7 us -> 59.3 us (level)
  no operation moved by 1% of the time
where the time goes in v6:
time: 59.3 us; the launch traced here: 59.1 us
  Pallas kernels  58.5 us (99%)
  between operations  0.64 us (1%)
    pallas_call x1, Pallas kernels, local(): pl.pallas_call(functools.partial(kernel, replicas, shards, parts), out_sh...  54.4 us
    pallas_call x1, Pallas kernels, local(): pl.pallas_call(write_out, out_shape=outs, in_specs=[pl.BlockSpec(memory_s...  4.06 us

profile of v6, /device:TPU:1, one launch (start us, length us, event | category | flops | bytes accessed | tf_op | source)
XLA Modules:
  0.0 59.1 jit_solution(11747682942191825087)
XLA Ops:
  0.6 54.4 %reduce_update_gather.1 = (f32[64,8192]{1,0:T(8,128)S(1)}, f32[64,8192]{1,0:T(8,128)S(1)}, f32[64,8192]{1,0:T(8,128)S(1)}, bf16[256,8192]{1,0:T(8,128)(2,1)S(1)}) custom-call(bf16[1,1,256,8192]{3,2,1,0:T(8,128)(2,1)} %grads.1, f32[64,8192]{1,0:T(8,128)} %master.1, f32[64,8192]{1,0:T(8,128)} %moment_one.1, f32[64,8192]{1,0:T(8,128)} %moment_two.1), custom_call_target="tpu_custom_call" | custom-call | tf_op jit(solution)/shard_map/reduce_update_gather/pallas_call | solution.py:357
  55.1 4.1 %write_out.1 = (f32[64,8192]{1,0:T(8,128)}, f32[64,8192]{1,0:T(8,128)}, f32[64,8192]{1,0:T(8,128)}, bf16[256,8192]{1,0:T(8,128)(2,1)}) custom-call(f32[64,8192]{1,0:T(8,128)S(1)} %get-tuple-element.8.refs_0_, f32[64,8192]{1,0:T(8,128)S(1)} %get-tuple-element.9.refs_1_, f32[64,8192]{1,0:T(8,128)S(1)} %get-tuple-element.10.refs_2_, ...), custom_call_target="tpu_custom_call" | custom-call | tf_op jit(solution)/shard_map/write_out/pallas_call | solution.py:388

commit v7 on v6

--- a/solution.py
+++ b/solution.py
@@ -124,10 +124,13 @@
     for n in range(2):
         start_core(n)
     states = []
-    for s, (source, target) in enumerate(((master, all_master), (moment_one, all_one), (moment_two, all_two))):
-        copy = pltpu.make_async_copy(source, target, state_sem.at[s])
-        copy.start()
-        states.append(copy)
+
+    def load_states():
+        for s, (source, target) in enumerate(((master, all_master), (moment_one, all_one), (moment_two, all_two))):
+            copy = pltpu.make_async_copy(source, target, state_sem.at[s])
+            copy.start()
+            states.append(copy)
+
     halving = {}
     shard_copies = {part: [] for part in range(parts)}
 
@@ -157,6 +160,8 @@
 
                 over_tiles(rows, stream, add)
                 start_halving(n, 0, q)
+            if n == 1:
+                load_states()
             return
         stage = step - 1
         for q in range(2):
@@ -210,12 +215,8 @@
                 held[m, tile(r), span(offset, c, wide)] = total.astype(jnp.bfloat16)
 
             over_tiles(rows, piece, finish)
-            join(m, stages - 1, q)
-        if part == 0:
-            for copy in states:
-                copy.wait()
-        for q in range(2):
-            offset = base(q, stages - 1)
+            while states:
+                states.pop().wait()
 
             def own_update(r, c, wide):
                 total = held[m, tile(r), span(offset, c, wide)].astype(jnp.float32)
@@ -225,19 +226,19 @@
                 own_weights[part, q, tile(r), pl.ds(c, wide)] = updated.astype(jnp.bfloat16)
 
             over_tiles(rows, piece, own_update)
-        for d in range(1, shards):
-            for q in range(2):
+            for d in range(1, shards):
                 spread[part, d, q] = remote(
-                    own_weights.at[part, q], held.at[m + d, :, aligned(base(q, stages - 1), piece)],
+                    own_weights.at[part, q], held.at[m + d, :, aligned(offset, piece)],
                     spread_send.at[part, d - 1, q], spread_recv.at[part, d - 1, q], me, lax.rem(at + d, shards),
                 )
                 sent.append(spread[part, d, q])
+            join(m, stages - 1, q)
 
     def update_rows(part, side, group, place):
         start = (bit[0] if side == 0 else 1 - bit[0]) * half
         m = part * shards
-        if side == 1 and group == 0 and place == 0:
-            pairs[m].wait_recv()
+        if side == 1 and group == 0:
+            pairs[m, place].wait_recv()
 
         def update(r, c, wide):
             r = pl.ds(group * 16, 16)
@@ -270,29 +271,30 @@
 
     def gather(m, step):
         part, j = divmod(m, shards)
+        block = chunk_rows(part, lax.rem(at + shards - j, shards))
         for q in range(2):
             if step > 0:
                 joining[m, stages - step, q].wait_recv()
             elif j > 0:
                 spread[part, j, q].wait_recv()
-            if step < stages and (j, step) != (0, 0):
-                join(m, stages - 1 - step, q)
-        if step < stages:
-            return
-        if j == 0:
-            target = total_pair.at[part]
+            if step < stages:
+                if (j, step) != (0, 0):
+                    join(m, stages - 1 - step, q)
+                continue
+            source = held.at[m, :, pl.ds(q * stream, stream)]
+            if j == 0:
+                target = total_pair.at[part, :, pl.ds(q * stream, stream)]
+            else:
+                target = weights_out.at[block, aligned(bit[0] * half + q * stream, stream)]
+                copy = pltpu.make_async_copy(source, target, store_sem.at[m, q])
+                copy.start()
+                local.append(copy)
+            pairs[m, q] = remote(source, target, pair_send.at[m, q], pair_recv.at[m, q], partner[0], at)
+            sent.append(pairs[m, q])
+        if step == stages and j == 0:
             todo.extend(
                 (part, side, group, place) for side in range(2) for group in range(rows // 16) for place in range(2)
             )
-        else:
-            target = weights_out.at[
-                chunk_rows(part, lax.rem(at + shards - j, shards)), aligned(bit[0] * half, half)
-            ]
-            copy = pltpu.make_async_copy(held.at[m], target, store_sem.at[m])
-            copy.start()
-            local.append(copy)
-        pairs[m] = remote(held.at[m], target, pair_send.at[m], pair_recv.at[m], partner[0], at)
-        sent.append(pairs[m])
 
     ahead = 2
 
@@ -321,7 +323,7 @@
     while todo:
         update_rows(*todo.pop(0))
 
-    for m, pair in pairs.items():
+    for (m, _), pair in pairs.items():
         if m % shards:
             pair.wait_recv()
     for copy in local:
@@ -371,14 +373,14 @@
             *[pltpu.VMEM(shape, jnp.bfloat16) for shape in halves * 2],
             sem((chunks,)),
             sem((3,)),
-            sem((chunks,)),
+            sem((chunks, 2)),
             sem((parts, 2, 4)),
             *[sem((chunks,))] * 2,
             *[sem((chunks, stages, 2))] * 2,
             *[sem((parts, shards - 1))] * 2,
             *[sem((parts, shards - 1, 2))] * 2,
             *[sem((chunks, stages, 2))] * 2,
-            *[sem((chunks,))] * 2,
+            *[sem((chunks, 2))] * 2,
         ],
         compiler_params=pltpu.CompilerParams(
             collective_id=0, has_side_effects=True, vmem_limit_bytes=28 * 1024 * 1024

time: 59.3 us -> 61.5 us (1.037)
  Pallas kernels: 58.5 us -> 60.7 us
    pallas_call x1, Pallas kernels: 54.4 us -> 56.6 us  [local(): pl.pallas_call(functools.partial(kernel, replicas, shards, parts), out_sh...]
where the time goes in v7:
time: 61.5 us; the launch traced here: 61.4 us
  Pallas kernels  60.7 us (99%)
  between operations  0.64 us (1%)
    pallas_call x1, Pallas kernels, local(): pl.pallas_call(functools.partial(kernel, replicas, shards, parts), out_sh...  56.6 us
    pallas_call x1, Pallas kernels, local(): pl.pallas_call(write_out, out_shape=outs, in_specs=[pl.BlockSpec(memory_s...  4.06 us

profile of v7, /device:TPU:1, one launch (start us, length us, event | category | flops | bytes accessed | tf_op | source)
XLA Modules:
  0.0 61.4 jit_solution(8280217923880060295)
XLA Ops:
  0.6 56.6 %reduce_update_gather.1 = (f32[64,8192]{1,0:T(8,128)S(1)}, f32[64,8192]{1,0:T(8,128)S(1)}, f32[64,8192]{1,0:T(8,128)S(1)}, bf16[256,8192]{1,0:T(8,128)(2,1)S(1)}) custom-call(bf16[1,1,256,8192]{3,2,1,0:T(8,128)(2,1)} %grads.1, f32[64,8192]{1,0:T(8,128)} %master.1, f32[64,8192]{1,0:T(8,128)} %moment_one.1, f32[64,8192]{1,0:T(8,128)} %moment_two.1), custom_call_target="tpu_custom_call" | custom-call | tf_op jit(solution)/shard_map/reduce_update_gather/pallas_call | solution.py:359
  57.3 4.1 %write_out.1 = (f32[64,8192]{1,0:T(8,128)}, f32[64,8192]{1,0:T(8,128)}, f32[64,8192]{1,0:T(8,128)}, bf16[256,8192]{1,0:T(8,128)(2,1)}) custom-call(f32[64,8192]{1,0:T(8,128)S(1)} %get-tuple-element.8.refs_0_, f32[64,8192]{1,0:T(8,128)S(1)} %get-tuple-element.9.refs_1_, f32[64,8192]{1,0:T(8,128)S(1)} %get-tuple-element.10.refs_2_, ...), custom_call_target="tpu_custom_call" | custom-call | tf_op jit(solution)/shard_map/write_out/pallas_call | solution.py:390
